TPU v7x, 128 devices: a whole 4x4x4 slice. The times are simulated.
128 devices in a mesh: face: 8 (over z, core), blk: 16 (over x, y).
Axes of the slice: x: 4, y: 4, z: 4, core: 2. Of those that a mesh axis runs over, the one named last changes fastest.
Arguments:
- fields: float32 [1024, 96, 2048], P('face', None, 'blk'), may hold values from -6 to 6
- weights: bfloat16 [128, 16, 8, 384, 128], P(('face', 'blk')), may hold values from -0.21875 to 0.21875
- src_tile: int32 [128, 16, 8], P(('face', 'blk')), may hold values from 0 to 127
- tgt_tile: int32 [128, 16, 8], P(('face', 'blk')), may hold values from 0 to 15, as said below
- counts: int32 [128, 16], P(('face', 'blk')), may hold values from 0 to 8, as said below
Outputs:
- remapped: float32 [2048, 96, 128], P(('face', 'blk'))
Inputs may be any that keep to these rules, and one draw needn't show every extreme that they name: `tgt_tile`: the 8 slots of one source block toward one device name distinct target tiles. `counts`: every source block has all 8 slots live toward at least one device; blocks of the first and last row of blocks have at least 4 live slots toward every device.
All inputs are finite; a program needn't handle non-finite values.
Results may differ from a plain program's by a relative error of at most 0.009.
Values may be sent and summed in bfloat16 or wider, within the bound.
A program may use at most 128 MiB of HBM per device.

v0:
```python
import jax
import jax.numpy as jnp
from jax import lax
from jax.sharding import PartitionSpec as P

TPD = 16


def extended(block, sides, width):
    for axis, dim in sides:
        count = lax.axis_size(axis)
        forward = [(i, i + 1) for i in range(count - 1)]
        forward.append((count - 1, 0))
        backward = [(target, source) for source, target in forward]
        low = lax.ppermute(
            lax.slice_in_dim(block, block.shape[dim] - width, None, axis=dim), axis, forward
        )
        high = lax.ppermute(lax.slice_in_dim(block, 0, width, axis=dim), axis, backward)
        block = jnp.concatenate([low, block, high], axis=dim)
    return block


def on_device(fields, weights, src_tile, tgt_tile, counts):
    row_count = fields.shape[1]
    width = fields.shape[2]
    padded = extended(fields, (("face", 0), ("blk", 2)), 1)
    grad_x = ((padded[2:, :, 1:-1] - padded[:-2, :, 1:-1]) * 0.5).astype(jnp.bfloat16)
    grad_y = ((padded[1:-1, :, 2:] - padded[1:-1, :, :-2]) * 0.5).astype(jnp.bfloat16)
    values = fields.astype(jnp.bfloat16)
    writers = src_tile.shape[1]
    capacity = src_tile.shape[2]
    tile_cells = weights.shape[4]
    slots = writers * capacity
    picked = src_tile.reshape(-1)
    flat_weights = weights.reshape(slots, weights.shape[3], tile_cells)
    products = jnp.einsum(
        "pmk,pkn->pmn",
        jnp.take(values, picked, axis=0),
        flat_weights[:, :width],
        preferred_element_type=jnp.float32,
    )
    products = products + jnp.einsum(
        "pmk,pkn->pmn",
        jnp.take(grad_x, picked, axis=0),
        flat_weights[:, width : 2 * width],
        preferred_element_type=jnp.float32,
    )
    products = products + jnp.einsum(
        "pmk,pkn->pmn",
        jnp.take(grad_y, picked, axis=0),
        flat_weights[:, 2 * width :],
        preferred_element_type=jnp.float32,
    )
    slot_ids = lax.broadcasted_iota(jnp.int32, (writers, capacity), 1)
    live_mask = (slot_ids < counts[0][:, None]).reshape(-1)
    partial_value = jnp.where(live_mask[:, None, None], products, 0.0).astype(jnp.bfloat16)
    arrived, arrived_targets = (
        lax.all_to_all(
            partial_value.reshape(writers, capacity, row_count * tile_cells),
            "blk",
            split_axis=0,
            concat_axis=0,
            tiled=True,
        ),
        lax.all_to_all(tgt_tile[0], "blk", split_axis=0, concat_axis=0, tiled=True),
    )
    one_hot = (
        arrived_targets.reshape(-1)[:, None] == lax.broadcasted_iota(jnp.int32, (slots, TPD), 1)
    ).astype(jnp.bfloat16)
    summed = jnp.einsum(
        "pt,pk->tk",
        one_hot,
        arrived.reshape(slots, row_count * tile_cells),
        preferred_element_type=jnp.float32,
    )
    return summed.reshape(TPD, row_count, tile_cells)


def solution(mesh):
    placed = (
        P("face", None, "blk"),
        P(("face", "blk"), None, None, None, None),
        P(("face", "blk"), None, None),
        P(("face", "blk"), None, None),
        P(("face", "blk"), None),
    )
    return jax.shard_map(
        on_device,
        mesh=mesh,
        in_specs=placed,
        out_specs=P(("face", "blk"), None, None),
        check_vma=False,
    )
```

profile of v0, /device:TPU:0, one launch (start us, length us, event | category | flops | bytes accessed | tf_op | source)
XLA Modules:
  0.0 165.7 jit_solution(12200479816117722648)
XLA Ops:
  0.0 0.8 fusion.33
  0.8 0.0 collective-permute-start.1
  0.8 3.6 %collective-permute-start = (f32[1,96,128]{2,1,0:T(8,128)S(1)}, f32[1,96,128]{2,1,0:T(8,128)S(1)}, u32[]{:S(2)}, u32[]{:S(2)}) collective-permute-start(f32[1,96,128]{2,1,0:T(8,128)S(1)} %get-tuple-element.11), channel_id=1, source_target_pairs={{16,0},{32,16},{48,32},{64,48},{80,64},{96,80},{112,96},{0,112},{1... | collective-permute-start | bytes 147464 | tf_op jit(solution)/shard_map/ppermute | solution.py:18
  4.4 1.4 copy.25
  5.8 7.0 %all-to-all-start = ((s32[16,1,8]{2,1,0:T(1,128)}), s32[16,1,8]{2,1,0:T(1,128)S(1)}, u32[]{:S(2)}, u32[]{:S(2)}) async-start(s32[16,1,8]{2,1,0:T(1,128)} %copy.25), calls=%async_computation | async-start | bytes 16384 | tf_op jit(solution)/shard_map/all_to_all | solution.py:65
  12.8 0.8 copy.26
  13.6 0.1 reshape.39
  13.7 0.7 iota_compare_fusion
  14.4 0.1 lt.26
  14.5 0.0 collective-permute-done.1
  14.5 0.6 constant_dynamic-update-slice_fusion.2
  15.2 0.0 collective-permute-done
  15.2 13.1 %constant_dynamic-update-slice_fusion.1 = (f32[130,96,128]{2,1,0:T(8,128)}, bf16[128,96,128]{2,1,0:T(8,128)(2,1)}, bf16[128,96,128]{2,1,0:T(8,128)(2,1)S(1)}) fusion(f32[130,96,128]{2,1,0:T(8,128)} %constant_dynamic-update-slice_fusion.2, f32[128,96,128]{2,1,0:T(8,128)} %param.7, f32[1,96,128]{2,1,0:T(8,128)S(1)} %collective-permute-done.1, ...), kind=kLoop, calls=%fused_computation.34 | loop fusion | flops 9437184 | bytes 18972672
  28.3 0.6 constant_dynamic-update-slice_fusion
  28.9 11.1 %fusion.32 = (f32[130,96,1]{2,1,0:T(8,128)}, f32[130,96,1]{2,1,0:T(8,128)}) fusion(f32[130,96,128]{2,1,0:T(8,128)} %constant_dynamic-update-slice_fusion), kind=kLoop, calls=%fused_computation.43 | loop fusion | bytes 199680 | tf_op jit(solution)/shard_map/slice | solution.py:18
  40.0 4.6 %copy.27 = f32[130,96,1]{1,0,2:T(8,128)S(1)} copy(f32[130,96,1]{2,1,0:T(8,128)} %get-tuple-element.6) | data formatting | bytes 99840 | tf_op jit(solution)/shard_map/slice | solution.py:18
  44.6 5.3 %collective-permute-start.2 = (f32[130,96,1]{1,0,2:T(8,128)S(1)}, f32[130,96,1]{1,0,2:T(8,128)S(1)}, u32[]{:S(2)}, u32[]{:S(2)}) collective-permute-start(f32[130,96,1]{1,0,2:T(8,128)S(1)} %copy.27), channel_id=1, source_target_pairs={{1,0},{2,1},{3,2},{4,3},{5,4},{6,5},{7,6},{8,7},{9,8},{10,9},{11,1... | collective-permute-start | bytes 149768 | tf_op jit(solution)/shard_map/ppermute | solution.py:18
  49.9 4.6 %copy.29 = f32[130,96,1]{1,0,2:T(8,128)S(1)} copy(f32[130,96,1]{2,1,0:T(8,128)} %get-tuple-element.7) | data formatting | bytes 99840 | tf_op jit(solution)/shard_map/slice | solution.py:16
  54.4 0.3 collective-permute-start.3
  54.7 4.5 %gather_fusion.1 = bf16[128,96,128]{2,1,0:T(8,128)(2,1)} fusion(bf16[128,96,128]{2,1,0:T(8,128)(2,1)} %get-tuple-element.9, s32[1024]{0:T(1024)S(1)} %pad_clamp_fusion), kind=kCustom, calls=%fused_computation.1.clone | custom fusion | bytes 6291968 | tf_op jit(solution)/shard_map/jit(_take)/gather | solution.py:44
  59.2 2.6 %gather_fusion = bf16[128,96,128]{2,1,0:T(8,128)(2,1)} fusion(bf16[128,96,128]{2,1,0:T(8,128)(2,1)S(1)} %get-tuple-element.10, s32[1024]{0:T(1024)S(1)} %pad_clamp_fusion), kind=kCustom, calls=%fused_computation.clone | custom fusion | bytes 6291968 | tf_op jit(solution)/shard_map/jit(_take)/gather | solution.py:38
  61.8 0.0 copy-start
  61.8 7.2 %fusion.8 = f32[128,96,128]{2,1,0:T(8,128)} fusion(bf16[128,384,128]{2,1,0:T(8,128)(2,1)} %bitcast.13, bf16[128,96,128]{2,1,0:T(8,128)(2,1)} %gather_fusion.1, pred[128]{0:T(512)(128)(4,1)S(1)} %compare_and_fusion), kind=kOutput, calls=%fused_computation.16 | convolution fusion | flops 404226048 | bytes 13631616 | tf_op jit(solution)/shard_map/pmk,pkn->pmn/dot_general | solution.py:42
  69.1 0.0 copy-done
  69.1 6.2 %fusion.10 = f32[128,96,128]{2,1,0:T(8,128)} fusion(bf16[128,384,128]{2,1,0:T(8,128)(2,1)} %bitcast.14, bf16[128,96,128]{2,1,0:T(8,128)(2,1)S(1)} %copy-done, pred[128]{0:T(512)(128)(4,1)S(1)} %compare_and_fusion), kind=kOutput, calls=%fused_computation.18 | convolution fusion | flops 404226048 | bytes 13631616 | tf_op jit(solution)/shard_map/pmk,pkn->pmn/dot_general | solution.py:36
  75.3 0.0 collective-permute-done.2
  75.3 4.1 %copy.28 = f32[130,96,1]{2,1,0:T(8,128)} copy(f32[130,96,1]{1,0,2:T(8,128)S(1)} %collective-permute-done.2) | data formatting | bytes 99840 | tf_op jit(solution)/shard_map/ppermute | solution.py:18
  79.4 0.0 collective-permute-done.3
  79.4 4.1 %copy.30 = f32[130,96,1]{2,1,0:T(8,128)} copy(f32[130,96,1]{1,0,2:T(8,128)S(1)} %collective-permute-done.3) | data formatting | bytes 99840 | tf_op jit(solution)/shard_map/ppermute | solution.py:15
  83.5 12.3 %fusion.2 = bf16[128,96,128]{2,1,0:T(8,128)(2,1)} fusion(f32[130,96,128]{2,1,0:T(8,128)} %constant_dynamic-update-slice_fusion, f32[130,96,1]{2,1,0:T(8,128)} %copy.30, f32[130,96,1]{2,1,0:T(8,128)} %copy.28), kind=kLoop, calls=%fused_computation.6 | loop fusion | flops 7864320 | bytes 9635328 | tf_op jit(solution)/shard_map/convert_element_type | solution.py:28
  95.8 3.0 %gather_fusion.2 = bf16[128,96,128]{2,1,0:T(8,128)(2,1)S(1)} fusion(bf16[128,96,128]{2,1,0:T(8,128)(2,1)} %fusion.2, s32[1024]{0:T(1024)S(1)} %pad_clamp_fusion), kind=kCustom, calls=%fused_computation.2.clone | custom fusion | bytes 6291968 | tf_op jit(solution)/shard_map/jit(_take)/gather | solution.py:50
  98.9 8.6 %select_convert_fusion = bf16[128,96,128]{2,1,0:T(8,128)(2,1)} fusion(f32[128,96,128]{2,1,0:T(8,128)} %fusion.10, f32[128,96,128]{2,1,0:T(8,128)} %fusion.8, pred[128]{0:T(512)(128)(4,1)S(1)} %lt.26, bf16[128,384,128]{2,1,0:T(8,128)(2,1)} %bitcast.15, bf16[128,96,128]{2,1,0:T(8,128)(2,1)S(1)} %gather_fusion.2, pred[128]{0:T(512)(128)(4,1)S(1)} %compare_and_fusion), kind=kOutput, calls=%fused_computation.13 | convolution fusion | flops 410517504 | bytes 23068928 | tf_op jit(solution)/shard_map/pmk,pkn->pmn/dot_general | solution.py:48
  107.5 5.6 %reshape.41 = bf16[16,8,12288]{2,1,0:T(8,128)(2,1)} reshape(bf16[128,96,128]{2,1,0:T(8,128)(2,1)} %select_convert_fusion) | data formatting | bytes 6291456 | tf_op jit(solution)/shard_map/reshape | solution.py:59
  113.1 0.0 all-to-all-done
  113.1 6.7 %all-to-all-start.1 = ((bf16[16,8,12288]{2,1,0:T(8,128)(2,1)}), bf16[16,8,12288]{2,1,0:T(8,128)(2,1)S(1)}, u32[]{:S(2)}, u32[]{:S(2)}) async-start(bf16[16,8,12288]{2,1,0:T(8,128)(2,1)} %reshape.41), calls=%async_computation.1 | async-start | bytes 6291456 | tf_op jit(solution)/shard_map/all_to_all | solution.py:58
  119.9 0.5 broadcast.25
  120.4 0.7 reduce.3
  121.0 0.1 eq.10
  121.1 37.8 %all-to-all-done.1 = bf16[16,8,12288]{2,1,0:T(8,128)(2,1)S(1)} async-done(((bf16[16,8,12288]{2,1,0:T(8,128)(2,1)}), bf16[16,8,12288]{2,1,0:T(8,128)(2,1)S(1)}, u32[]{:S(2)}, u32[]{:S(2)}) %all-to-all-start.1) | async-done | bytes 3145760 | tf_op jit(solution)/shard_map/all_to_all | solution.py:58
  159.0 2.8 %copy.31 = bf16[128,12288]{0,1:T(8,128)(2,1)} copy(bf16[128,12288]{1,0:T(8,128)(2,1)S(1)} %bitcast.11) | data formatting | bytes 6291456 | tf_op jit(solution)/shard_map/reshape | solution.py:73
  161.7 2.8 %fusion.26 = f32[16,96,128]{2,0,1:T(8,128)S(1)} fusion(bf16[96,128,128]{2,1,0:T(8,128)(2,1)} %bitcast.12, s32[128]{0:T(128)S(1)} %eq.10), kind=kOutput, calls=%fused_computation.32 | convolution fusion | flops 50333696 | bytes 3932672 | tf_op jit(solution)/shard_map/pt,pk->tk/dot_general | solution.py:70
  164.5 1.1 copy.32
  (3 shorter events, 0.0 us)
Async XLA Ops:
  0.8 13.7 %collective-permute-start.1 = (f32[1,96,128]{2,1,0:T(8,128)S(1)}, f32[1,96,128]{2,1,0:T(8,128)S(1)}, u32[]{:S(2)}, u32[]{:S(2)}) collective-permute-start(f32[1,96,128]{2,1,0:T(8,128)S(1)} %get-tuple-element.12), channel_id=1, source_target_pairs={{0,16},{16,32},{32,48},{48,64},{64,80},{80,96},{96,112},{112,0},{1... | collective-permute-start | bytes 147464 | tf_op jit(solution)/shard_map/ppermute | solution.py:15
  0.8 14.3 %collective-permute-start = (f32[1,96,128]{2,1,0:T(8,128)S(1)}, f32[1,96,128]{2,1,0:T(8,128)S(1)}, u32[]{:S(2)}, u32[]{:S(2)}) collective-permute-start(f32[1,96,128]{2,1,0:T(8,128)S(1)} %get-tuple-element.11), channel_id=1, source_target_pairs={{16,0},{32,16},{48,32},{64,48},{80,64},{96,80},{112,96},{0,112},{1... | collective-permute-start | bytes 147464 | tf_op jit(solution)/shard_map/ppermute | solution.py:18
  5.8 107.4 %all-to-all-start = ((s32[16,1,8]{2,1,0:T(1,128)}), s32[16,1,8]{2,1,0:T(1,128)S(1)}, u32[]{:S(2)}, u32[]{:S(2)}) async-start(s32[16,1,8]{2,1,0:T(1,128)} %copy.25), calls=%async_computation | async-start | bytes 16384 | tf_op jit(solution)/shard_map/all_to_all | solution.py:65
  44.6 30.7 %collective-permute-start.2 = (f32[130,96,1]{1,0,2:T(8,128)S(1)}, f32[130,96,1]{1,0,2:T(8,128)S(1)}, u32[]{:S(2)}, u32[]{:S(2)}) collective-permute-start(f32[130,96,1]{1,0,2:T(8,128)S(1)} %copy.27), channel_id=1, source_target_pairs={{1,0},{2,1},{3,2},{4,3},{5,4},{6,5},{7,6},{8,7},{9,8},{10,9},{11,1... | collective-permute-start | bytes 149768 | tf_op jit(solution)/shard_map/ppermute | solution.py:18
  54.4 25.0 %collective-permute-start.3 = (f32[130,96,1]{1,0,2:T(8,128)S(1)}, f32[130,96,1]{1,0,2:T(8,128)S(1)}, u32[]{:S(2)}, u32[]{:S(2)}) collective-permute-start(f32[130,96,1]{1,0,2:T(8,128)S(1)} %copy.29), channel_id=1, source_target_pairs={{0,1},{1,2},{2,3},{3,4},{4,5},{5,6},{6,7},{7,8},{8,9},{9,10},{10,1... | collective-permute-start | bytes 149768 | tf_op jit(solution)/shard_map/ppermute | solution.py:15
  61.8 7.2 %copy-start = (bf16[128,96,128]{2,1,0:T(8,128)(2,1)S(1)}, bf16[128,96,128]{2,1,0:T(8,128)(2,1)}, u32[]{:S(2)}) copy-start(bf16[128,96,128]{2,1,0:T(8,128)(2,1)} %gather_fusion) | copy-start | bytes 9437188
  113.1 45.8 %all-to-all-start.1 = ((bf16[16,8,12288]{2,1,0:T(8,128)(2,1)}), bf16[16,8,12288]{2,1,0:T(8,128)(2,1)S(1)}, u32[]{:S(2)}, u32[]{:S(2)}) async-start(bf16[16,8,12288]{2,1,0:T(8,128)(2,1)} %reshape.41), calls=%async_computation.1 | async-start | bytes 6291456 | tf_op jit(solution)/shard_map/all_to_all | solution.py:58
where the time goes:
time: 168 us; the launch traced here: 166 us
  local copies, waits for them, and re-layouts  53.1 us (32%)
  waiting for transfers between devices  37.8 us (22%)
  other arithmetic  26.8 us (16%)
  matrix products  24.9 us (15%)
  starting transfers between devices  22.9 us (14%)
    all_to_all x1, waiting for transfers between devices, on_device(): lax.all_to_all(partial_value.reshape(writers, capacity, row_count * tile_...  37.8 us
    slice x3, local copies, waits for them, and re-layouts, extended(): lax.slice_in_dim(block, 0, width, axis=dim)  16.5 us
    unnamed x1, other arithmetic  13.1 us
    convert_element_type x1, other arithmetic, on_device(): ((padded[1:-1, :, 2:] - padded[1:-1, :, :-2]) * 0.5).astype(jnp.bfloat16)  12.3 us
    ppermute x2, starting transfers between devices, extended(): lax.ppermute(lax.slice_in_dim(block, 0, width, axis=dim), axis, backward)  8.89 us
    dot_general x1, matrix products, on_device(): jnp.einsum('pmk,pkn->pmn', jnp.take(grad_y, picked, axis=0), flat_weights...  8.64 us
    dot_general x1, matrix products, on_device(): jnp.einsum('pmk,pkn->pmn', jnp.take(grad_x, picked, axis=0), flat_weights...  7.24 us
    all_to_all x1, starting transfers between devices, on_device(): lax.all_to_all(tgt_tile[0], 'blk', split_axis=0, concat_axis=0, tiled=True)  7.03 us
  transfers between devices with their start and end apart: 6, of which 1 were waited for; matrix products, arithmetic and copies ran while one was open for 59% of the time, Pallas kernels for 0%

commit v1 on v0

v1 whole, which is shorter than its diff:
```python
import jax
import jax.numpy as jnp
from jax import lax
from jax.experimental import pallas as pl
from jax.experimental.pallas import tpu as pltpu
from jax.sharding import PartitionSpec as P

MESH = pl.DeviceIdType.MESH
SIDE = 4
CHUNKS = 8
ROUTES = 2
PARTS = 2
STEPS = {"x+": (1, 0), "x-": (3, 0), "y+": (0, 1), "y-": (0, 3)}
TREES = (
    {
        (0, 1): "x-", (0, 2): "y+", (0, 3): "y+", (1, 0): "x-", (1, 1): "y+",
        (1, 2): "y+", (1, 3): "x-", (2, 0): "x+", (2, 1): "x+", (2, 2): "x-",
        (2, 3): "x-", (3, 0): "x+", (3, 1): "y-", (3, 2): "y-", (3, 3): "y+",
    },
    {
        (0, 1): "y-", (0, 2): "y-", (0, 3): "x+", (1, 0): "x-", (1, 1): "y-",
        (1, 2): "y+", (1, 3): "y+", (2, 0): "x-", (2, 1): "x+", (2, 2): "x+",
        (2, 3): "x-", (3, 0): "x+", (3, 1): "x+", (3, 2): "y-", (3, 3): "y-",
    },
)
PLAN = (
    ((3, 3), ()),
    ((2, 2), ()),
    ((2, 0), ()),
    ((1, 1), ()),
    ((2, 3), ()),
    ((0, 2), ()),
    ((2, 1), ()),
    ((3, 2), ((1, (3, 2), 0), (1, (3, 2), 1),)),
    ((1, 2), ((0, (1, 2), 0), (0, (1, 2), 1),)),
    ((0, 3), ()),
    ((0, 1), ()),
    ((1, 0), ()),
    ((3, 0), ()),
    ((0, 0), ()),
    ((3, 1), ()),
    ((1, 3), (
        (0, (1, 3), 0), (0, (3, 1), 0), (1, (1, 3), 0), (1, (3, 1), 0),
        (0, (3, 1), 1), (1, (1, 3), 1), (1, (3, 1), 1), (0, (1, 3), 1),
        (0, (0, 0), 0), (1, (0, 0), 0), (0, (3, 0), 0), (0, (0, 3), 0),
        (1, (0, 1), 0), (1, (1, 0), 0), (0, (3, 0), 1), (0, (0, 3), 1),
        (1, (0, 1), 1), (1, (1, 0), 1),
    )),
)
LAST = (
    (1, (0, 1), 0), (1, (1, 0), 0), (0, (0, 3), 0), (0, (3, 0), 0),
    (1, (0, 1), 1), (1, (1, 0), 1), (0, (0, 3), 1), (0, (3, 0), 1),
)
TABLES_AFTER = 6
ORDER = tuple(entry[0] for entry in PLAN)


def parent(route, o):
    dx, dy = STEPS[TREES[route][o]]
    return ((o[0] + dx) % SIDE, (o[1] + dy) % SIDE)


def children(route, o):
    return [v for v in TREES[route] if parent(route, v) == o]


INNER = [[v for v in tree if children(route, v)] for route, tree in enumerate(TREES)]
LEAVES = [[v for v in tree if not children(route, v)] for route, tree in enumerate(TREES)]


def coded(values):
    word = sum(v << (2 * k) for k, v in enumerate(values))
    return word - (1 << 32) if word >= 1 << 31 else word


def kernel(
    ints_in, fields_ref, weights_ref, out_ref,
    ints, cells, wts, part, col_own, col_send, col_recv, turns, tab_send, tab_recv, tab, sums, sums_in,
    *rest,
):
    raw_in = {}
    for route in range(ROUTES):
        for v in LEAVES[route]:
            raw_in[route, v] = rest[len(raw_in)]
    send_sem, recv_sem, field_sem, weight_sem, tab_sem, ints_sem = rest[len(raw_in):]
    bx, rows, width = fields_ref.shape
    cap, writers = ints.shape[1] // 2, ints.shape[2]
    tiles = out_ref.shape[0]
    height = rows // ROUTES
    share = tiles // PARTS
    faces = lax.axis_size("face")
    face = lax.axis_index("face")
    blk = lax.axis_index("blk")
    px, py = blk // SIDE, lax.rem(blk, SIDE)

    def at(a, b):
        return lax.rem(px + a, SIDE) * SIDE + lax.rem(py + b, SIDE)

    def writer(o):
        return at((SIDE - o[0]) % SIDE, (SIDE - o[1]) % SIDE)

    near = {name: (face, at(*step)) for name, step in STEPS.items()}
    up, down = lax.rem(face + 1, faces), lax.rem(face + faces - 1, faces)
    right, left = lax.rem(blk + 1, writers), lax.rem(blk + writers - 1, writers)
    barrier = pltpu.get_barrier_semaphore()
    greeted = [(up, blk), (down, blk), (face, left), (face, right)] + list(near.values())
    for peer in greeted:
        pl.semaphore_signal(barrier, inc=1, device_id=peer, device_id_type=MESH)

    fields_in = []
    step = bx // CHUNKS
    for i in range(CHUNKS):
        copy = pltpu.make_async_copy(
            fields_ref.at[pl.ds(i * step, step)], cells.at[pl.ds(1 + i * step, step)], field_sem.at[i]
        )
        copy.start()
        fields_in.append(copy)
    ints_copy = pltpu.make_async_copy(ints_in, ints, ints_sem)
    ints_copy.start()
    weights_in = [
        pltpu.make_async_copy(weights_ref.at[0, writer(o)], wts.at[k, :, pl.ds(0, weights_ref.shape[3])], weight_sem.at[k])
        for k, o in enumerate(ORDER)
    ]

    messages = []

    def message(src, dst, peer):
        i = len(messages)
        messages.append(
            pltpu.make_async_remote_copy(
                src_ref=src, dst_ref=dst, send_sem=send_sem.at[i], recv_sem=recv_sem.at[i],
                device_id=peer, device_id_type=MESH,
            )
        )
        return messages[i]

    halo = [
        message(fields_ref.at[bx - 1], cells.at[0], (up, blk)),
        message(fields_ref.at[0], cells.at[bx + 1], (down, blk)),
        message(col_send.at[0], col_recv.at[0], (face, right)),
        message(col_send.at[1], col_recv.at[1], (face, left)),
    ]
    tables = [message(tab_send, tab_recv.at[i], near[name]) for i, name in enumerate(STEPS)]
    raw, summed = {}, {}
    for route, tree in enumerate(TREES):
        rs = pl.ds(route * height, height)
        for v in LEAVES[route]:
            raw[route, v] = message(
                part.at[ORDER.index(v), pl.ds(0, cap), rs], raw_in[route, v].at[pl.ds(0, cap)], near[tree[v]]
            )
        for i, v in enumerate(INNER[route]):
            for h in range(PARTS):
                some = pl.ds(h * share, share)
                summed[route, v, h] = message(sums.at[route, i, some], sums_in.at[route, i, some], near[tree[v]])

    depth = weights_ref.shape[3]
    group = width // cap

    def clear(k, carry):
        for c in range(cap):
            wts[k, c, pl.ds(depth, width), :] = jnp.zeros((width, wts.shape[3]), wts.dtype)
        return carry

    lax.fori_loop(0, writers, clear, 0)

    pl.semaphore_wait(barrier, len(greeted))
    halo[0].start()
    halo[1].start()

    lanes = lax.broadcasted_iota(jnp.int32, (rows, width), 1)
    edges = (jnp.zeros((rows, width), jnp.float32), jnp.zeros((rows, width), jnp.float32))
    for i in range(CHUNKS):
        fields_in[i].wait()
        if i >= CHUNKS // 2:
            weights_in[i - CHUNKS // 2].start()

        def pick(j, edges):
            x = i * step + j
            turned = pltpu.roll(cells[1 + x], lax.rem(x + 1, width), 1)
            return (
                jnp.where(lanes == x, turned, edges[0]),
                jnp.where(lanes == lax.rem(x + 1, width), turned, edges[1]),
            )

        edges = lax.fori_loop(0, step, pick, edges, unroll=4)
    for i in range(2):
        col_own[i] = edges[i]
        col_send[i] = edges[i].astype(col_send.dtype)
    halo[2].start()
    halo[3].start()
    for copy in weights_in[CHUNKS - CHUNKS // 2:]:
        copy.start()

    ints_copy.wait()
    lane = lax.broadcasted_iota(jnp.int32, (1, 128), 1)

    def make_row(d, carry):
        row = jnp.full((1, 128), cap, jnp.int32)
        for c in range(cap):
            target = jnp.where(c < ints[0, 2 * cap, d], ints[0, cap + c, d], 127)
            row = jnp.where(lane == target, c, row)
        tab_send[pl.ds(d, 1), :] = row
        return carry

    lax.fori_loop(0, writers, make_row, 0)
    for copy in tables:
        copy.start()
    for buf in raw_in.values():
        buf[cap] = jnp.zeros((height, width), buf.dtype)
    for k, o in enumerate(ORDER):
        if o not in LEAVES[0] or o not in LEAVES[1]:
            part[k, cap] = jnp.zeros((rows, width), part.dtype)
    for copy in halo:
        copy.wait_recv()
    turns[:, pl.ds(0, width)] = (col_own[0] - col_recv[0].astype(jnp.float32)).astype(turns.dtype)
    turns[:, pl.ds(width, width)] = (col_recv[1].astype(jnp.float32) - col_own[1]).astype(turns.dtype)
    group_row = lax.broadcasted_iota(jnp.int32, (group, wts.shape[3]), 0)
    turn_row = lax.broadcasted_iota(jnp.int32, (2 * width, width), 0)

    def read_tables():
        for copy in tables:
            copy.wait_recv()
        sources = [tab_recv.at[i] for i in range(len(STEPS))] + [tab_send]
        copies = [pltpu.make_async_copy(src, tab.at[i], tab_sem.at[i]) for i, src in enumerate(sources)]
        for copy in copies:
            copy.start()
        for copy in copies:
            copy.wait()

    here = set()

    def gather(route, o, h, store):
        d = writer(o)
        k = ORDER.index(o)
        rs = pl.ds(route * height, height)
        below = children(route, o)
        plain = [v for v in below if v in LEAVES[route]]
        dense = [INNER[route].index(v) for v in below if v in INNER[route]]
        if o == (0, 0):
            dense = []
        for v in plain:
            if (route, v) not in here:
                raw[route, v].wait_recv()
                here.add((route, v))
        for i in dense:
            summed[route, INNER[route][i], h].wait_recv()
        ways = list(STEPS)

        def one(j, carry):
            t = h * share + j
            total = part[k, tab[len(ways), d, t], rs, :].astype(jnp.float32)
            for v in plain:
                slot = tab[ways.index(TREES[route][v]), d, t]
                total += raw_in[route, v][slot].astype(jnp.float32)
            for i in dense:
                total += sums_in[route, i, t].astype(jnp.float32)
            store(t, total)
            return carry

        lax.fori_loop(0, share, one, 0, unroll=4)

    def follow(route, o, h):
        if o == (0, 0):
            def store(t, total):
                out_ref[t, pl.ds(route * height, height), :] = total * 0.5

            for part_of in range(PARTS):
                gather(route, o, part_of, store)
        else:
            i = INNER[route].index(o)

            def store(t, total):
                sums[route, i, t] = total.astype(sums.dtype)

            gather(route, o, h, store)
            summed[route, o, h].start()

    code_x = jnp.int32(coded([(SIDE - o[0]) % SIDE for o in ORDER]))
    code_y = jnp.int32(coded([(SIDE - o[1]) % SIDE for o in ORDER]))

    def products(k, carry):
        d = at((code_x >> (2 * k)) & 3, (code_y >> (2 * k)) & 3)
        pltpu.make_async_copy(weights_ref.at[0, 0], wts.at[k, :, pl.ds(0, depth)], weight_sem.at[k]).wait()
        where_from = jnp.full((1, width), -1, jnp.int32)
        for c in range(cap):
            x = ints[0, c, d]
            where_from = jnp.where(lane == c * group, x, where_from)
            where_from = jnp.where(lane == c * group + group - 1, width + lax.rem(x + 1, width), where_from)
            first = wts[k, c, pl.ds(2 * width, group), :].astype(jnp.float32)
            final = wts[k, c, pl.ds(3 * width - group, group), :].astype(jnp.float32)
            edge = jnp.where(group_row == 0, first, jnp.where(group_row == group - 1, final, 0.0))
            wts[k, c, pl.ds(depth + c * group, group), :] = edge.astype(wts.dtype)
        chosen = jnp.where(turn_row == where_from, 1.0, 0.0).astype(jnp.bfloat16)
        turned = jnp.dot(turns[...], chosen, preferred_element_type=jnp.float32).astype(jnp.bfloat16)
        for c in range(cap):
            x = ints[0, c, d]
            value = cells[x + 1]
            grad_x = cells[x + 2] - cells[x]
            grad_y = pltpu.roll(value, width - 1, 1) - pltpu.roll(value, 1, 1)
            stacked = jnp.concatenate([value + value, grad_x, grad_y], axis=1).astype(jnp.bfloat16)
            stacked = jnp.concatenate([stacked, turned], axis=1)
            product = jnp.dot(stacked, wts[k, c], preferred_element_type=jnp.float32)
            part[k, c] = product.astype(part.dtype)

        for i, (o, sums_after) in enumerate(PLAN):
            ready = [raw[route, o] for route in range(ROUTES) if o in LEAVES[route]]
            if i == len(PLAN) - 1:
                sums_after = ()
            if ready or sums_after or i == TABLES_AFTER:
                @pl.when(k == i)
                def _():
                    for copy in ready:
                        copy.start()
                    if i == TABLES_AFTER:
                        read_tables()
                    for entry in sums_after:
                        follow(*entry)
        return carry

    lax.fori_loop(0, len(PLAN), products, 0)
    for entry in PLAN[-1][1]:
        follow(*entry)
    for route, v, h in LAST:
        rs = pl.ds(route * height, height)
        i = INNER[route].index(v)
        summed[route, v, h].wait_recv()

        def add(j, carry):
            t = h * share + j
            out_ref[t, rs, :] += sums_in[route, i, t].astype(jnp.float32) * 0.5
            return carry

        lax.fori_loop(0, share, add, 0, unroll=4)
    for copy in messages:
        copy.wait_send()


def on_device(fields, weights, src_tile, tgt_tile, counts):
    bx, rows, width = fields.shape
    _, writers, cap, depth, tile_cells = weights.shape
    tiles = 16
    height = rows // ROUTES
    leaves = sum(len(some) for some in LEAVES)
    inner = len(INNER[0])
    messages = 8 + leaves + ROUTES * inner * PARTS
    bf16 = jnp.bfloat16
    ints = jnp.concatenate(
        [jnp.swapaxes(src_tile, 1, 2), jnp.swapaxes(tgt_tile, 1, 2), counts[:, None, :]], axis=1
    )
    return pl.pallas_call(
        kernel,
        out_shape=jax.ShapeDtypeStruct((tiles, rows, tile_cells), jnp.float32),
        in_specs=[pl.BlockSpec(memory_space=pl.ANY)] * 3,
        out_specs=pl.BlockSpec(memory_space=pltpu.VMEM),
        scratch_shapes=[
            pltpu.SMEM((1, 2 * cap + 1, writers), jnp.int32),
            pltpu.VMEM((bx + 2, rows, width), jnp.float32),
            pltpu.VMEM((writers, cap, depth + width, tile_cells), bf16),
            pltpu.VMEM((writers, cap + 1, rows, tile_cells), bf16),
            pltpu.VMEM((2, rows, width), jnp.float32),
            pltpu.VMEM((2, rows, width), bf16),
            pltpu.VMEM((2, rows, width), bf16),
            pltpu.VMEM((rows, 2 * width), bf16),
            pltpu.VMEM((writers, 128), jnp.int32),
            pltpu.VMEM((len(STEPS), writers, 128), jnp.int32),
            pltpu.SMEM((len(STEPS) + 1, writers, 128), jnp.int32),
            pltpu.VMEM((ROUTES, inner, tiles, height, tile_cells), bf16),
            pltpu.VMEM((ROUTES, inner, tiles, height, tile_cells), bf16),
        ]
        + [pltpu.VMEM((cap + 1, height, tile_cells), bf16)] * leaves
        + [
            pltpu.SemaphoreType.DMA((messages,)),
            pltpu.SemaphoreType.DMA((messages,)),
            pltpu.SemaphoreType.DMA((CHUNKS,)),
            pltpu.SemaphoreType.DMA((writers,)),
            pltpu.SemaphoreType.DMA((len(STEPS) + 1,)),
            pltpu.SemaphoreType.DMA,
        ],
        compiler_params=pltpu.CompilerParams(
            collective_id=0, has_side_effects=True, vmem_limit_bytes=52 * 1024 * 1024
        ),
        cost_estimate=pl.CostEstimate(flops=1208000000, bytes_accessed=19700000, transcendentals=0),
    )(ints, fields, weights)


def solution(mesh):
    placed = (
        P("face", None, "blk"),
        P(("face", "blk"), None, None, None, None),
        P(("face", "blk"), None, None),
        P(("face", "blk"), None, None),
        P(("face", "blk"), None),
    )
    return jax.shard_map(
        on_device,
        mesh=mesh,
        in_specs=placed,
        out_specs=P(("face", "blk"), None, None),
        check_vma=False,
    )
```

time: 168 us -> 41.5 us (0.25); the launches traced: 166 us -> 41.2 us
  local copies, waits for them, and re-layouts: 53.1 us -> 0.88 us
  Pallas kernels: 0 us -> 39.6 us
  waiting for transfers between devices: 37.8 us -> 0 us
  other arithmetic: 26.8 us -> 0.72 us
  matrix products: 24.9 us -> 0 us
  starting transfers between devices: 22.9 us -> 0 us
    pallas_call x0 -> x1, Pallas kernels: none -> 39.6 us  [on_device(): pl.pallas_call(kernel, out_shape=jax.ShapeDtypeStruct((tiles, rows, tile_...]
    all_to_all x2 -> x0, waiting for transfers between devices: 37.8 us -> none  [the longest x1 37.8 us: on_device(): lax.all_to_all(partial_value.reshape(writers, capacity, row_count * tile_...]
    dot_general x4 -> x0, matrix products: 24.9 us -> none  [the longest x1 8.64 us: on_device(): jnp.einsum('pmk,pkn->pmn', jnp.take(grad_y, picked, axis=0), flat_weights...]
    slice x4 -> x0, local copies, waits for them, and re-layouts: 21 us -> none  [the longest x3 16.5 us: extended(): lax.slice_in_dim(block, 0, width, axis=dim)]
    all_to_all x2 -> x0, starting transfers between devices: 13.7 us -> none  [the longest x1 7.03 us: on_device(): lax.all_to_all(tgt_tile[0], 'blk', split_axis=0, concat_axis=0, tiled=True)]
    unnamed x1 -> x0, other arithmetic: 13.1 us -> none
    convert_element_type x1 -> x0, other arithmetic: 12.3 us -> none  [on_device(): ((padded[1:-1, :, 2:] - padded[1:-1, :, :-2]) * 0.5).astype(jnp.bfloat16)]
    gather x3 -> x0, local copies, waits for them, and re-layouts: 10.2 us -> none  [the longest x1 4.48 us: on_device(): jnp.take(grad_x, picked, axis=0)]
  transfers between devices with their start and end apart: 6 -> 0, of which waited for: 1 -> 0; matrix products, arithmetic and copies ran while one was open for 59% -> 0% of each run, Pallas kernels for 0% -> 0%
where the time goes in v1:
time: 41.5 us; the launch traced here: 41.2 us
  Pallas kernels  39.6 us (95%)
  local copies, waits for them, and re-layouts  0.88 us (2%)
  other arithmetic  0.72 us (2%)
    pallas_call x1, Pallas kernels, on_device(): pl.pallas_call(kernel, out_shape=jax.ShapeDtypeStruct((tiles, rows, tile_...  39.6 us
    unnamed x1, local copies, waits for them, and re-layouts  0.88 us

profile of v1, /device:TPU:0, one launch (start us, length us, event | category | flops | bytes accessed | tf_op | source)
XLA Modules:
  0.0 41.2 jit_solution(3074783384708767188)
XLA Ops:
  0.0 0.7 %pad_add_fusion.ints_in = s32[1,17,16]{2,1,0:T(8,128)S(1)} fusion(s32[1,1,16]{2,1,0:T(1,128)} %bitcast.5, s32[1,8,16]{2,1,0:T(8,128)} %bitcast.3, s32[1,8,16]{2,1,0:T(8,128)} %bitcast.4), kind=kLoop, calls=%fused_computation | loop fusion | flops 544 | bytes 2176 | tf_op jit(solution)/shard_map/concatenate | solution.py:347
  0.7 39.6 %shard_map.55 = f32[16,96,128]{2,1,0:T(8,128)S(1)} custom-call(s32[1,17,16]{2,1,0:T(8,128)S(1)} %pad_add_fusion.ints_in, f32[128,96,128]{2,1,0:T(8,128)} %fields_ref.1, bf16[1,16,8,384,128]{4,3,2,1,0:T(8,128)(2,1)} %weights_ref.1), custom_call_target="tpu_custom_call" | custom-call | flops 1208000000 | bytes 19700000 | tf_op jit(solution)/shard_map/pallas_call | solution.py:350
  40.3 0.9 %copy.7 = f32[16,96,128]{2,1,0:T(8,128)} copy(f32[16,96,128]{2,1,0:T(8,128)S(1)} %shard_map.55) | data formatting | bytes 1572864

commit v2 on v1

--- a/solution.py
+++ b/solution.py
@@ -13,45 +13,49 @@
 STEPS = {"x+": (1, 0), "x-": (3, 0), "y+": (0, 1), "y-": (0, 3)}
 TREES = (
     {
-        (0, 1): "x-", (0, 2): "y+", (0, 3): "y+", (1, 0): "x-", (1, 1): "y+",
-        (1, 2): "y+", (1, 3): "x-", (2, 0): "x+", (2, 1): "x+", (2, 2): "x-",
-        (2, 3): "x-", (3, 0): "x+", (3, 1): "y-", (3, 2): "y-", (3, 3): "y+",
+        (0, 1): "y-", (0, 2): "y+", (0, 3): "y+", (1, 0): "x-", (1, 1): "x-",
+        (1, 2): "y-", (1, 3): "x-", (2, 0): "y+", (2, 1): "x-", (2, 2): "y-",
+        (2, 3): "x+", (3, 0): "x+", (3, 1): "x+", (3, 2): "y+", (3, 3): "x+",
     },
     {
-        (0, 1): "y-", (0, 2): "y-", (0, 3): "x+", (1, 0): "x-", (1, 1): "y-",
-        (1, 2): "y+", (1, 3): "y+", (2, 0): "x-", (2, 1): "x+", (2, 2): "x+",
-        (2, 3): "x-", (3, 0): "x+", (3, 1): "x+", (3, 2): "y-", (3, 3): "y-",
+        (0, 1): "y-", (0, 2): "x+", (0, 3): "y+", (1, 0): "x-", (1, 1): "y-",
+        (1, 2): "y-", (1, 3): "y+", (2, 0): "x+", (2, 1): "x-", (2, 2): "x-",
+        (2, 3): "x+", (3, 0): "x+", (3, 1): "y-", (3, 2): "y+", (3, 3): "y+",
     },
 )
 PLAN = (
-    ((3, 3), ()),
+    ((2, 0), ()),
     ((2, 2), ()),
-    ((2, 0), ()),
-    ((1, 1), ()),
-    ((2, 3), ()),
     ((0, 2), ()),
     ((2, 1), ()),
-    ((3, 2), ((1, (3, 2), 0), (1, (3, 2), 1),)),
-    ((1, 2), ((0, (1, 2), 0), (0, (1, 2), 1),)),
+    ((3, 1), ()),
+    ((3, 2), ((0, (2, 1), 0), (0, (2, 1), 1),)),
+    ((1, 2), ((1, (1, 2), 0), (1, (1, 2), 1),)),
+    ((2, 3), ()),
+    ((1, 3), ()),
+    ((3, 3), ()),
     ((0, 3), ()),
-    ((0, 1), ()),
-    ((1, 0), ()),
+    ((1, 1), (
+        (0, (1, 1), 0), (0, (3, 3), 0), (1, (1, 1), 0), (0, (1, 1), 1),
+        (0, (3, 3), 1),
+    )),
+    ((1, 0), (
+        (1, (3, 3), 0), (1, (3, 3), 1), (1, (1, 1), 1),
+    )),
     ((3, 0), ()),
-    ((0, 0), ()),
-    ((3, 1), ()),
-    ((1, 3), (
-        (0, (1, 3), 0), (0, (3, 1), 0), (1, (1, 3), 0), (1, (3, 1), 0),
-        (0, (3, 1), 1), (1, (1, 3), 1), (1, (3, 1), 1), (0, (1, 3), 1),
-        (0, (0, 0), 0), (1, (0, 0), 0), (0, (3, 0), 0), (0, (0, 3), 0),
-        (1, (0, 1), 0), (1, (1, 0), 0), (0, (3, 0), 1), (0, (0, 3), 1),
-        (1, (0, 1), 1), (1, (1, 0), 1),
+    ((0, 1), (
+        (0, (0, 1), 0), (0, (0, 3), 0), (1, (1, 0), 0),
+    )),
+    ((0, 0), (
+        (1, (3, 0), 0), (0, (0, 1), 1), (0, (0, 3), 1), (1, (1, 0), 1),
+        (1, (3, 0), 1), (0, (0, 0), 0), (1, (0, 0), 0),
     )),
 )
 LAST = (
-    (1, (0, 1), 0), (1, (1, 0), 0), (0, (0, 3), 0), (0, (3, 0), 0),
-    (1, (0, 1), 1), (1, (1, 0), 1), (0, (0, 3), 1), (0, (3, 0), 1),
+    (0, (0, 3), 0), (1, (1, 0), 0), (1, (3, 0), 0), (0, (0, 1), 0),
+    (0, (0, 3), 1), (1, (1, 0), 1), (1, (3, 0), 1), (0, (0, 1), 1),
 )
-TABLES_AFTER = 6
+TABLES_AFTER = 4
 ORDER = tuple(entry[0] for entry in PLAN)
 
 
@@ -75,7 +79,7 @@
 
 def kernel(
     ints_in, fields_ref, weights_ref, out_ref,
-    ints, cells, wts, part, col_own, col_send, col_recv, turns, tab_send, tab_recv, tab, sums, sums_in,
+    ints, cells, wts, part, col_own, col_send, col_recv, turns, early, tab_send, tab_recv, tab, sums, sums_in,
     *rest,
 ):
     raw_in = {}
@@ -210,12 +214,58 @@
     for k, o in enumerate(ORDER):
         if o not in LEAVES[0] or o not in LEAVES[1]:
             part[k, cap] = jnp.zeros((rows, width), part.dtype)
-    for copy in halo:
-        copy.wait_recv()
+    group_row = lax.broadcasted_iota(jnp.int32, (group, wts.shape[3]), 0)
+    turn_row = lax.broadcasted_iota(jnp.int32, (2 * width, width), 0)
+    code_x = jnp.int32(coded([(SIDE - o[0]) % SIDE for o in ORDER]))
+    code_y = jnp.int32(coded([(SIDE - o[1]) % SIDE for o in ORDER]))
+
+    def writer_at(k):
+        return at((code_x >> (2 * k)) & 3, (code_y >> (2 * k)) & 3)
+
+    def stack(x):
+        value = cells[x + 1]
+        grad_x = cells[x + 2] - cells[x]
+        grad_y = pltpu.roll(value, width - 1, 1) - pltpu.roll(value, 1, 1)
+        return jnp.concatenate([value + value, grad_x, grad_y], axis=1).astype(jnp.bfloat16)
+
+    def turn(d):
+        where_from = jnp.full((1, width), -1, jnp.int32)
+        for c in range(cap):
+            x = ints[0, c, d]
+            where_from = jnp.where(lane == c * group, x, where_from)
+            where_from = jnp.where(lane == c * group + group - 1, width + lax.rem(x + 1, width), where_from)
+        chosen = jnp.where(turn_row == where_from, 1.0, 0.0).astype(jnp.bfloat16)
+        return jnp.dot(turns[...], chosen, preferred_element_type=jnp.float32).astype(jnp.bfloat16)
+
+    def edge_rows(k):
+        for c in range(cap):
+            first = wts[k, c, pl.ds(2 * width, group), :].astype(jnp.float32)
+            final = wts[k, c, pl.ds(3 * width - group, group), :].astype(jnp.float32)
+            edge = jnp.where(group_row == 0, first, jnp.where(group_row == group - 1, final, 0.0))
+            wts[k, c, pl.ds(depth + c * group, group), :] = edge.astype(wts.dtype)
+
+    halo[0].wait_recv()
+    halo[1].wait_recv()
+    weights_in[0].wait()
+    edge_rows(0)
+    d_first = writer(ORDER[0])
+
+    def begin(c, carry):
+        early[c] = jnp.dot(stack(ints[0, c, d_first]), wts[0, c, pl.ds(0, depth), :], preferred_element_type=jnp.float32)
+        return carry
+
+    lax.fori_loop(0, cap, begin, 0, unroll=4)
+    halo[2].wait_recv()
+    halo[3].wait_recv()
     turns[:, pl.ds(0, width)] = (col_own[0] - col_recv[0].astype(jnp.float32)).astype(turns.dtype)
     turns[:, pl.ds(width, width)] = (col_recv[1].astype(jnp.float32) - col_own[1]).astype(turns.dtype)
-    group_row = lax.broadcasted_iota(jnp.int32, (group, wts.shape[3]), 0)
-    turn_row = lax.broadcasted_iota(jnp.int32, (2 * width, width), 0)
+    turned = turn(d_first)
+    for c in range(cap):
+        product = early[c] + jnp.dot(turned, wts[0, c, pl.ds(depth, width), :], preferred_element_type=jnp.float32)
+        part[0, c] = product.astype(part.dtype)
+    for route in range(ROUTES):
+        if ORDER[0] in LEAVES[route]:
+            raw[route, ORDER[0]].start()
 
     def read_tables():
         for copy in tables:
@@ -257,7 +307,7 @@
             store(t, total)
             return carry
 
-        lax.fori_loop(0, share, one, 0, unroll=4)
+        lax.fori_loop(0, share, one, 0, unroll=8)
 
     def follow(route, o, h):
         if o == (0, 0):
@@ -275,34 +325,19 @@
             gather(route, o, h, store)
             summed[route, o, h].start()
 
-    code_x = jnp.int32(coded([(SIDE - o[0]) % SIDE for o in ORDER]))
-    code_y = jnp.int32(coded([(SIDE - o[1]) % SIDE for o in ORDER]))
-
-    def products(k, carry):
-        d = at((code_x >> (2 * k)) & 3, (code_y >> (2 * k)) & 3)
+    def products(k, turned):
+        d = writer_at(k)
         pltpu.make_async_copy(weights_ref.at[0, 0], wts.at[k, :, pl.ds(0, depth)], weight_sem.at[k]).wait()
-        where_from = jnp.full((1, width), -1, jnp.int32)
+        edge_rows(k)
+        later = turn(writer_at(lax.rem(k + 1, len(PLAN))))
         for c in range(cap):
-            x = ints[0, c, d]
-            where_from = jnp.where(lane == c * group, x, where_from)
-            where_from = jnp.where(lane == c * group + group - 1, width + lax.rem(x + 1, width), where_from)
-            first = wts[k, c, pl.ds(2 * width, group), :].astype(jnp.float32)
-            final = wts[k, c, pl.ds(3 * width - group, group), :].astype(jnp.float32)
-            edge = jnp.where(group_row == 0, first, jnp.where(group_row == group - 1, final, 0.0))
-            wts[k, c, pl.ds(depth + c * group, group), :] = edge.astype(wts.dtype)
-        chosen = jnp.where(turn_row == where_from, 1.0, 0.0).astype(jnp.bfloat16)
-        turned = jnp.dot(turns[...], chosen, preferred_element_type=jnp.float32).astype(jnp.bfloat16)
-        for c in range(cap):
-            x = ints[0, c, d]
-            value = cells[x + 1]
-            grad_x = cells[x + 2] - cells[x]
-            grad_y = pltpu.roll(value, width - 1, 1) - pltpu.roll(value, 1, 1)
-            stacked = jnp.concatenate([value + value, grad_x, grad_y], axis=1).astype(jnp.bfloat16)
-            stacked = jnp.concatenate([stacked, turned], axis=1)
+            stacked = jnp.concatenate([stack(ints[0, c, d]), turned], axis=1)
             product = jnp.dot(stacked, wts[k, c], preferred_element_type=jnp.float32)
             part[k, c] = product.astype(part.dtype)
 
         for i, (o, sums_after) in enumerate(PLAN):
+            if i == 0:
+                continue
             ready = [raw[route, o] for route in range(ROUTES) if o in LEAVES[route]]
             if i == len(PLAN) - 1:
                 sums_after = ()
@@ -315,9 +350,9 @@
                         read_tables()
                     for entry in sums_after:
                         follow(*entry)
-        return carry
-
-    lax.fori_loop(0, len(PLAN), products, 0)
+        return later
+
+    lax.fori_loop(1, len(PLAN), products, turn(writer(ORDER[1])))
     for entry in PLAN[-1][1]:
         follow(*entry)
     for route, v, h in LAST:
@@ -330,7 +365,7 @@
             out_ref[t, rs, :] += sums_in[route, i, t].astype(jnp.float32) * 0.5
             return carry
 
-        lax.fori_loop(0, share, add, 0, unroll=4)
+        lax.fori_loop(0, share, add, 0, unroll=8)
     for copy in messages:
         copy.wait_send()
 
@@ -361,6 +396,7 @@
             pltpu.VMEM((2, rows, width), bf16),
             pltpu.VMEM((2, rows, width), bf16),
             pltpu.VMEM((rows, 2 * width), bf16),
+            pltpu.VMEM((cap, rows, tile_cells), jnp.float32),
             pltpu.VMEM((writers, 128), jnp.int32),
             pltpu.VMEM((len(STEPS), writers, 128), jnp.int32),
             pltpu.SMEM((len(STEPS) + 1, writers, 128), jnp.int32),

time: 41.5 us -> 41.5 us (level)
  no operation moved by 1% of the time
where the time goes in v2:
time: 41.5 us; the launch traced here: 41.3 us
  Pallas kernels  39.7 us (96%)
  local copies, waits for them, and re-layouts  0.88 us (2%)
  other arithmetic  0.72 us (2%)
    pallas_call x1, Pallas kernels, on_device(): pl.pallas_call(kernel, out_shape=jax.ShapeDtypeStruct((tiles, rows, tile_...  39.7 us
    unnamed x1, local copies, waits for them, and re-layouts  0.88 us

profile of v2, /device:TPU:0, one launch (start us, length us, event | category | flops | bytes accessed | tf_op | source)
XLA Modules:
  0.0 41.3 jit_solution(8818872263868799474)
XLA Ops:
  0.0 0.7 %pad_add_fusion.ints_in = s32[1,17,16]{2,1,0:T(8,128)S(1)} fusion(s32[1,1,16]{2,1,0:T(1,128)} %bitcast.5, s32[1,8,16]{2,1,0:T(8,128)} %bitcast.3, s32[1,8,16]{2,1,0:T(8,128)} %bitcast.4), kind=kLoop, calls=%fused_computation | loop fusion | flops 544 | bytes 2176 | tf_op jit(solution)/shard_map/concatenate | solution.py:382
  0.7 39.7 %shard_map.55 = f32[16,96,128]{2,1,0:T(8,128)S(1)} custom-call(s32[1,17,16]{2,1,0:T(8,128)S(1)} %pad_add_fusion.ints_in, f32[128,96,128]{2,1,0:T(8,128)} %fields_ref.1, bf16[1,16,8,384,128]{4,3,2,1,0:T(8,128)(2,1)} %weights_ref.1), custom_call_target="tpu_custom_call" | custom-call | flops 1208000000 | bytes 19700000 | tf_op jit(solution)/shard_map/pallas_call | solution.py:385
  40.5 0.9 %copy.7 = f32[16,96,128]{2,1,0:T(8,128)} copy(f32[16,96,128]{2,1,0:T(8,128)S(1)} %shard_map.55) | data formatting | bytes 1572864

commit v3 on v2

--- a/solution.py
+++ b/solution.py
@@ -330,10 +330,15 @@
         pltpu.make_async_copy(weights_ref.at[0, 0], wts.at[k, :, pl.ds(0, depth)], weight_sem.at[k]).wait()
         edge_rows(k)
         later = turn(writer_at(lax.rem(k + 1, len(PLAN))))
-        for c in range(cap):
-            stacked = jnp.concatenate([stack(ints[0, c, d]), turned], axis=1)
-            product = jnp.dot(stacked, wts[k, c], preferred_element_type=jnp.float32)
-            part[k, c] = product.astype(part.dtype)
+        for c in range(0, cap, 2):
+            pair = [jnp.concatenate([stack(ints[0, c + i, d]), turned], axis=1) for i in range(2)]
+            both = jnp.dot(
+                jnp.concatenate(pair, axis=0),
+                jnp.concatenate([wts[k, c], wts[k, c + 1]], axis=1),
+                preferred_element_type=jnp.float32,
+            )
+            part[k, c] = both[:rows, :width].astype(part.dtype)
+            part[k, c + 1] = both[rows:, width:].astype(part.dtype)
 
         for i, (o, sums_after) in enumerate(PLAN):
             if i == 0:

time: 41.5 us -> 41.5 us (level)
  no operation moved by 1% of the time
where the time goes in v3:
time: 41.5 us; the launch traced here: 41.3 us
  Pallas kernels  39.7 us (96%)
  local copies, waits for them, and re-layouts  0.88 us (2%)
  other arithmetic  0.72 us (2%)
    pallas_call x1, Pallas kernels, on_device(): pl.pallas_call(kernel, out_shape=jax.ShapeDtypeStruct((tiles, rows, tile_...  39.7 us
    unnamed x1, local copies, waits for them, and re-layouts  0.88 us

profile of v3, /device:TPU:0, one launch (start us, length us, event | category | flops | bytes accessed | tf_op | source)
XLA Modules:
  0.0 41.3 jit_solution(3976592852598270502)
XLA Ops:
  0.0 0.7 %pad_add_fusion.ints_in = s32[1,17,16]{2,1,0:T(8,128)S(1)} fusion(s32[1,1,16]{2,1,0:T(1,128)} %bitcast.5, s32[1,8,16]{2,1,0:T(8,128)} %bitcast.3, s32[1,8,16]{2,1,0:T(8,128)} %bitcast.4), kind=kLoop, calls=%fused_computation | loop fusion | flops 544 | bytes 2176 | tf_op jit(solution)/shard_map/concatenate | solution.py:387
  0.7 39.7 %shard_map.55 = f32[16,96,128]{2,1,0:T(8,128)S(1)} custom-call(s32[1,17,16]{2,1,0:T(8,128)S(1)} %pad_add_fusion.ints_in, f32[128,96,128]{2,1,0:T(8,128)} %fields_ref.1, bf16[1,16,8,384,128]{4,3,2,1,0:T(8,128)(2,1)} %weights_ref.1), custom_call_target="tpu_custom_call" | custom-call | flops 1208000000 | bytes 19700000 | tf_op jit(solution)/shard_map/pallas_call | solution.py:390
  40.5 0.9 %copy.7 = f32[16,96,128]{2,1,0:T(8,128)} copy(f32[16,96,128]{2,1,0:T(8,128)S(1)} %shard_map.55) | data formatting | bytes 1572864

commit v4 on v2

--- a/solution.py
+++ b/solution.py
@@ -9,53 +9,58 @@
 SIDE = 4
 CHUNKS = 8
 ROUTES = 2
-PARTS = 2
+PARTS = 4
 STEPS = {"x+": (1, 0), "x-": (3, 0), "y+": (0, 1), "y-": (0, 3)}
 TREES = (
     {
-        (0, 1): "y-", (0, 2): "y+", (0, 3): "y+", (1, 0): "x-", (1, 1): "x-",
-        (1, 2): "y-", (1, 3): "x-", (2, 0): "y+", (2, 1): "x-", (2, 2): "y-",
-        (2, 3): "x+", (3, 0): "x+", (3, 1): "x+", (3, 2): "y+", (3, 3): "x+",
+        (0, 1): "x+", (0, 2): "y+", (0, 3): "y+", (1, 0): "x-", (1, 1): "y-",
+        (1, 2): "y-", (1, 3): "y+", (2, 0): "x-", (2, 1): "x-", (2, 2): "x+",
+        (2, 3): "x+", (3, 0): "x+", (3, 1): "y+", (3, 2): "y+", (3, 3): "x+",
     },
     {
-        (0, 1): "y-", (0, 2): "x+", (0, 3): "y+", (1, 0): "x-", (1, 1): "y-",
-        (1, 2): "y-", (1, 3): "y+", (2, 0): "x+", (2, 1): "x-", (2, 2): "x-",
+        (0, 1): "y-", (0, 2): "y-", (0, 3): "x-", (1, 0): "x-", (1, 1): "x-",
+        (1, 2): "y-", (1, 3): "y-", (2, 0): "x+", (2, 1): "x-", (2, 2): "x-",
         (2, 3): "x+", (3, 0): "x+", (3, 1): "y-", (3, 2): "y+", (3, 3): "y+",
     },
 )
 PLAN = (
+    ((3, 1), ()),
+    ((2, 2), ()),
+    ((2, 1), ()),
+    ((1, 3), ()),
+    ((0, 1), ()),
+    ((2, 3), ()),
+    ((0, 2), ()),
+    ((0, 3), ()),
+    ((1, 2), ()),
+    ((3, 2), (
+        (0, (3, 2), 0), (0, (3, 2), 1), (0, (3, 2), 2), (1, (1, 2), 0),
+        (1, (1, 2), 1), (1, (1, 2), 2), (0, (3, 2), 3), (1, (1, 2), 3),
+    )),
     ((2, 0), ()),
-    ((2, 2), ()),
-    ((0, 2), ()),
-    ((2, 1), ()),
-    ((3, 1), ()),
-    ((3, 2), ((0, (2, 1), 0), (0, (2, 1), 1),)),
-    ((1, 2), ((1, (1, 2), 0), (1, (1, 2), 1),)),
-    ((2, 3), ()),
-    ((1, 3), ()),
+    ((1, 1), ()),
+    ((1, 0), ()),
+    ((3, 0), ()),
     ((3, 3), ()),
-    ((0, 3), ()),
-    ((1, 1), (
-        (0, (1, 1), 0), (0, (3, 3), 0), (1, (1, 1), 0), (0, (1, 1), 1),
-        (0, (3, 3), 1),
-    )),
-    ((1, 0), (
-        (1, (3, 3), 0), (1, (3, 3), 1), (1, (1, 1), 1),
-    )),
-    ((3, 0), ()),
-    ((0, 1), (
-        (0, (0, 1), 0), (0, (0, 3), 0), (1, (1, 0), 0),
-    )),
     ((0, 0), (
-        (1, (3, 0), 0), (0, (0, 1), 1), (0, (0, 3), 1), (1, (1, 0), 1),
-        (1, (3, 0), 1), (0, (0, 0), 0), (1, (0, 0), 0),
+        (0, (1, 1), 0), (1, (3, 3), 0), (0, (1, 1), 1), (1, (3, 3), 1),
+        (0, (1, 1), 2), (1, (3, 3), 2), (1, (1, 1), 0), (0, (1, 1), 3),
+        (0, (3, 3), 0), (1, (3, 3), 3), (1, (1, 1), 1), (0, (3, 3), 1),
+        (1, (1, 1), 2), (0, (3, 3), 2), (1, (1, 1), 3), (0, (3, 3), 3),
+        (1, (0, 0), 0), (0, (0, 0), 0), (0, (1, 0), 0), (1, (3, 0), 0),
+        (1, (0, 1), 0), (0, (0, 3), 0), (0, (1, 0), 1), (1, (3, 0), 1),
+        (1, (0, 1), 1), (0, (0, 3), 1), (0, (1, 0), 2), (1, (3, 0), 2),
+        (1, (0, 1), 2), (0, (0, 3), 2), (0, (1, 0), 3), (1, (3, 0), 3),
+        (1, (0, 1), 3), (0, (0, 3), 3),
     )),
 )
 LAST = (
-    (0, (0, 3), 0), (1, (1, 0), 0), (1, (3, 0), 0), (0, (0, 1), 0),
-    (0, (0, 3), 1), (1, (1, 0), 1), (1, (3, 0), 1), (0, (0, 1), 1),
+    (1, (0, 1), 0), (0, (0, 3), 0), (0, (1, 0), 0), (1, (3, 0), 0),
+    (1, (0, 1), 1), (0, (0, 3), 1), (0, (1, 0), 1), (1, (3, 0), 1),
+    (1, (0, 1), 2), (0, (0, 3), 2), (0, (1, 0), 2), (1, (3, 0), 2),
+    (1, (0, 1), 3), (0, (0, 3), 3), (0, (1, 0), 3), (1, (3, 0), 3),
 )
-TABLES_AFTER = 4
+TABLES_AFTER = 8
 ORDER = tuple(entry[0] for entry in PLAN)
 
 
@@ -307,7 +312,7 @@
             store(t, total)
             return carry
 
-        lax.fori_loop(0, share, one, 0, unroll=8)
+        lax.fori_loop(0, share, one, 0, unroll=4)
 
     def follow(route, o, h):
         if o == (0, 0):
@@ -365,7 +370,7 @@
             out_ref[t, rs, :] += sums_in[route, i, t].astype(jnp.float32) * 0.5
             return carry
 
-        lax.fori_loop(0, share, add, 0, unroll=8)
+        lax.fori_loop(0, share, add, 0, unroll=4)
     for copy in messages:
         copy.wait_send()
 

time: 41.5 us -> 41.7 us (level)
  no operation moved by 1% of the time
where the time goes in v4:
time: 41.7 us; the launch traced here: 41.6 us
  Pallas kernels  39.9 us (96%)
  local copies, waits for them, and re-layouts  0.88 us (2%)
  other arithmetic  0.72 us (2%)
    pallas_call x1, Pallas kernels, on_device(): pl.pallas_call(kernel, out_shape=jax.ShapeDtypeStruct((tiles, rows, tile_...  39.9 us
    unnamed x1, local copies, waits for them, and re-layouts  0.88 us

profile of v4, /device:TPU:0, one launch (start us, length us, event | category | flops | bytes accessed | tf_op | source)
XLA Modules:
  0.0 41.6 jit_solution(12240216082949823114)
XLA Ops:
  0.0 0.7 %pad_add_fusion.ints_in = s32[1,17,16]{2,1,0:T(8,128)S(1)} fusion(s32[1,1,16]{2,1,0:T(1,128)} %bitcast.5, s32[1,8,16]{2,1,0:T(8,128)} %bitcast.3, s32[1,8,16]{2,1,0:T(8,128)} %bitcast.4), kind=kLoop, calls=%fused_computation | loop fusion | flops 544 | bytes 2176 | tf_op jit(solution)/shard_map/concatenate | solution.py:387
  0.7 39.9 %shard_map.55 = f32[16,96,128]{2,1,0:T(8,128)S(1)} custom-call(s32[1,17,16]{2,1,0:T(8,128)S(1)} %pad_add_fusion.ints_in, f32[128,96,128]{2,1,0:T(8,128)} %fields_ref.1, bf16[1,16,8,384,128]{4,3,2,1,0:T(8,128)(2,1)} %weights_ref.1), custom_call_target="tpu_custom_call" | custom-call | flops 1208000000 | bytes 19700000 | tf_op jit(solution)/shard_map/pallas_call | solution.py:390
  40.7 0.9 %copy.7 = f32[16,96,128]{2,1,0:T(8,128)} copy(f32[16,96,128]{2,1,0:T(8,128)S(1)} %shard_map.55) | data formatting | bytes 1572864

commit v5 on v2

--- a/solution.py
+++ b/solution.py
@@ -103,14 +103,6 @@
     def writer(o):
         return at((SIDE - o[0]) % SIDE, (SIDE - o[1]) % SIDE)
 
-    near = {name: (face, at(*step)) for name, step in STEPS.items()}
-    up, down = lax.rem(face + 1, faces), lax.rem(face + faces - 1, faces)
-    right, left = lax.rem(blk + 1, writers), lax.rem(blk + writers - 1, writers)
-    barrier = pltpu.get_barrier_semaphore()
-    greeted = [(up, blk), (down, blk), (face, left), (face, right)] + list(near.values())
-    for peer in greeted:
-        pl.semaphore_signal(barrier, inc=1, device_id=peer, device_id_type=MESH)
-
     fields_in = []
     step = bx // CHUNKS
     for i in range(CHUNKS):
@@ -119,6 +111,14 @@
         )
         copy.start()
         fields_in.append(copy)
+    near = {name: (face, at(*step)) for name, step in STEPS.items()}
+    up, down = lax.rem(face + 1, faces), lax.rem(face + faces - 1, faces)
+    right, left = lax.rem(blk + 1, writers), lax.rem(blk + writers - 1, writers)
+    barrier = pltpu.get_barrier_semaphore()
+    greeted = [(up, blk), (down, blk), (face, left), (face, right)] + list(near.values())
+    for peer in greeted:
+        pl.semaphore_signal(barrier, inc=1, device_id=peer, device_id_type=MESH)
+
     ints_copy = pltpu.make_async_copy(ints_in, ints, ints_sem)
     ints_copy.start()
     weights_in = [
@@ -167,29 +167,34 @@
 
     lax.fori_loop(0, writers, clear, 0)
 
+    lanes = lax.broadcasted_iota(jnp.int32, (rows, width), 1)
+
+    def pack_edges():
+        edges = (jnp.zeros((rows, width), jnp.float32), jnp.zeros((rows, width), jnp.float32))
+        for i in range(CHUNKS):
+            fields_in[i].wait()
+            if i >= CHUNKS // 2:
+                weights_in[i - CHUNKS // 2].start()
+
+            def pick(j, edges):
+                x = i * step + j
+                turned = pltpu.roll(cells[1 + x], lax.rem(x + 1, width), 1)
+                return (
+                    jnp.where(lanes == x, turned, edges[0]),
+                    jnp.where(lanes == lax.rem(x + 1, width), turned, edges[1]),
+                )
+
+            edges = lax.fori_loop(0, step, pick, edges, unroll=4)
+        for i in range(2):
+            col_own[i] = edges[i]
+            col_send[i] = edges[i].astype(col_send.dtype)
+
+    core = lax.rem(face, 2)
+    pl.when(core == 0)(pack_edges)
     pl.semaphore_wait(barrier, len(greeted))
     halo[0].start()
     halo[1].start()
-
-    lanes = lax.broadcasted_iota(jnp.int32, (rows, width), 1)
-    edges = (jnp.zeros((rows, width), jnp.float32), jnp.zeros((rows, width), jnp.float32))
-    for i in range(CHUNKS):
-        fields_in[i].wait()
-        if i >= CHUNKS // 2:
-            weights_in[i - CHUNKS // 2].start()
-
-        def pick(j, edges):
-            x = i * step + j
-            turned = pltpu.roll(cells[1 + x], lax.rem(x + 1, width), 1)
-            return (
-                jnp.where(lanes == x, turned, edges[0]),
-                jnp.where(lanes == lax.rem(x + 1, width), turned, edges[1]),
-            )
-
-        edges = lax.fori_loop(0, step, pick, edges, unroll=4)
-    for i in range(2):
-        col_own[i] = edges[i]
-        col_send[i] = edges[i].astype(col_send.dtype)
+    pl.when(core != 0)(pack_edges)
     halo[2].start()
     halo[3].start()
     for copy in weights_in[CHUNKS - CHUNKS // 2:]:
@@ -228,14 +233,16 @@
         grad_y = pltpu.roll(value, width - 1, 1) - pltpu.roll(value, 1, 1)
         return jnp.concatenate([value + value, grad_x, grad_y], axis=1).astype(jnp.bfloat16)
 
-    def turn(d):
+    def pick_edges(d):
         where_from = jnp.full((1, width), -1, jnp.int32)
         for c in range(cap):
             x = ints[0, c, d]
             where_from = jnp.where(lane == c * group, x, where_from)
             where_from = jnp.where(lane == c * group + group - 1, width + lax.rem(x + 1, width), where_from)
-        chosen = jnp.where(turn_row == where_from, 1.0, 0.0).astype(jnp.bfloat16)
-        return jnp.dot(turns[...], chosen, preferred_element_type=jnp.float32).astype(jnp.bfloat16)
+        return jnp.where(turn_row == where_from, 1.0, 0.0).astype(jnp.bfloat16)
+
+    def turn(picked):
+        return jnp.dot(turns[...], picked, preferred_element_type=jnp.float32).astype(jnp.bfloat16)
 
     def edge_rows(k):
         for c in range(cap):
@@ -255,11 +262,12 @@
         return carry
 
     lax.fori_loop(0, cap, begin, 0, unroll=4)
+    picked = pick_edges(d_first)
     halo[2].wait_recv()
     halo[3].wait_recv()
     turns[:, pl.ds(0, width)] = (col_own[0] - col_recv[0].astype(jnp.float32)).astype(turns.dtype)
     turns[:, pl.ds(width, width)] = (col_recv[1].astype(jnp.float32) - col_own[1]).astype(turns.dtype)
-    turned = turn(d_first)
+    turned = turn(picked)
     for c in range(cap):
         product = early[c] + jnp.dot(turned, wts[0, c, pl.ds(depth, width), :], preferred_element_type=jnp.float32)
         part[0, c] = product.astype(part.dtype)
@@ -329,7 +337,7 @@
         d = writer_at(k)
         pltpu.make_async_copy(weights_ref.at[0, 0], wts.at[k, :, pl.ds(0, depth)], weight_sem.at[k]).wait()
         edge_rows(k)
-        later = turn(writer_at(lax.rem(k + 1, len(PLAN))))
+        later = turn(pick_edges(writer_at(lax.rem(k + 1, len(PLAN)))))
         for c in range(cap):
             stacked = jnp.concatenate([stack(ints[0, c, d]), turned], axis=1)
             product = jnp.dot(stacked, wts[k, c], preferred_element_type=jnp.float32)
@@ -352,7 +360,7 @@
                         follow(*entry)
         return later
 
-    lax.fori_loop(1, len(PLAN), products, turn(writer(ORDER[1])))
+    lax.fori_loop(1, len(PLAN), products, turn(pick_edges(writer(ORDER[1]))))
     for entry in PLAN[-1][1]:
         follow(*entry)
     for route, v, h in LAST:

time: 41.5 us -> 40.3 us (0.971)
  Pallas kernels: 39.7 us -> 38.5 us
    pallas_call x1, Pallas kernels: 39.7 us -> 38.5 us  [on_device(): pl.pallas_call(kernel, out_shape=jax.ShapeDtypeStruct((tiles, rows, tile_...]
where the time goes in v5:
time: 40.3 us; the launch traced here: 40.2 us
  Pallas kernels  38.5 us (96%)
  local copies, waits for them, and re-layouts  0.88 us (2%)
  other arithmetic  0.72 us (2%)
    pallas_call x1, Pallas kernels, on_device(): pl.pallas_call(kernel, out_shape=jax.ShapeDtypeStruct((tiles, rows, tile_...  38.5 us
    unnamed x1, local copies, waits for them, and re-layouts  0.88 us

profile of v5, /device:TPU:0, one launch (start us, length us, event | category | flops | bytes accessed | tf_op | source)
XLA Modules:
  0.0 40.2 jit_solution(7815816000372412862)
XLA Ops:
  0.0 0.7 %pad_add_fusion.ints_in = s32[1,17,16]{2,1,0:T(8,128)S(1)} fusion(s32[1,1,16]{2,1,0:T(1,128)} %bitcast.5, s32[1,8,16]{2,1,0:T(8,128)} %bitcast.3, s32[1,8,16]{2,1,0:T(8,128)} %bitcast.4), kind=kLoop, calls=%fused_computation | loop fusion | flops 544 | bytes 2176 | tf_op jit(solution)/shard_map/concatenate | solution.py:390
  0.7 38.5 %shard_map.55 = f32[16,96,128]{2,1,0:T(8,128)S(1)} custom-call(s32[1,17,16]{2,1,0:T(8,128)S(1)} %pad_add_fusion.ints_in, f32[128,96,128]{2,1,0:T(8,128)} %fields_ref.1, bf16[1,16,8,384,128]{4,3,2,1,0:T(8,128)(2,1)} %weights_ref.1), custom_call_target="tpu_custom_call" | custom-call | flops 1208000000 | bytes 19700000 | tf_op jit(solution)/shard_map/pallas_call | solution.py:393
  39.3 0.9 %copy.7 = f32[16,96,128]{2,1,0:T(8,128)} copy(f32[16,96,128]{2,1,0:T(8,128)S(1)} %shard_map.55) | data formatting | bytes 1572864

commit v6 on v5

--- a/solution.py
+++ b/solution.py
@@ -165,16 +165,36 @@
             wts[k, c, pl.ds(depth, width), :] = jnp.zeros((width, wts.shape[3]), wts.dtype)
         return carry
 
-    lax.fori_loop(0, writers, clear, 0)
+    def clear_all():
+        lax.fori_loop(0, writers, clear, 0)
 
     lanes = lax.broadcasted_iota(jnp.int32, (rows, width), 1)
+    lane = lax.broadcasted_iota(jnp.int32, (1, 128), 1)
+
+    def make_tables():
+        ints_copy.wait()
+
+        def make_row(d, carry):
+            row = jnp.full((1, 128), cap, jnp.int32)
+            for c in range(cap):
+                target = jnp.where(c < ints[0, 2 * cap, d], ints[0, cap + c, d], 127)
+                row = jnp.where(lane == target, c, row)
+            tab_send[pl.ds(d, 1), :] = row
+            return carry
+
+        lax.fori_loop(0, writers, make_row, 0)
+        for buf in raw_in.values():
+            buf[cap] = jnp.zeros((height, width), buf.dtype)
+        for k, o in enumerate(ORDER):
+            if o not in LEAVES[0] or o not in LEAVES[1]:
+                part[k, cap] = jnp.zeros((rows, width), part.dtype)
 
     def pack_edges():
         edges = (jnp.zeros((rows, width), jnp.float32), jnp.zeros((rows, width), jnp.float32))
         for i in range(CHUNKS):
             fields_in[i].wait()
-            if i >= CHUNKS // 2:
-                weights_in[i - CHUNKS // 2].start()
+            if i == CHUNKS - 1:
+                weights_in[0].start()
 
             def pick(j, edges):
                 x = i * step + j
@@ -190,35 +210,30 @@
             col_send[i] = edges[i].astype(col_send.dtype)
 
     core = lax.rem(face, 2)
-    pl.when(core == 0)(pack_edges)
+
+    @pl.when(core == 0)
+    def _():
+        make_tables()
+        clear_all()
+        pack_edges()
+
     pl.semaphore_wait(barrier, len(greeted))
     halo[0].start()
     halo[1].start()
-    pl.when(core != 0)(pack_edges)
+
+    @pl.when(core != 0)
+    def _():
+        make_tables()
+        pack_edges()
+
     halo[2].start()
     halo[3].start()
-    for copy in weights_in[CHUNKS - CHUNKS // 2:]:
+    for copy in weights_in[1:]:
         copy.start()
-
-    ints_copy.wait()
-    lane = lax.broadcasted_iota(jnp.int32, (1, 128), 1)
-
-    def make_row(d, carry):
-        row = jnp.full((1, 128), cap, jnp.int32)
-        for c in range(cap):
-            target = jnp.where(c < ints[0, 2 * cap, d], ints[0, cap + c, d], 127)
-            row = jnp.where(lane == target, c, row)
-        tab_send[pl.ds(d, 1), :] = row
-        return carry
-
-    lax.fori_loop(0, writers, make_row, 0)
     for copy in tables:
         copy.start()
-    for buf in raw_in.values():
-        buf[cap] = jnp.zeros((height, width), buf.dtype)
-    for k, o in enumerate(ORDER):
-        if o not in LEAVES[0] or o not in LEAVES[1]:
-            part[k, cap] = jnp.zeros((rows, width), part.dtype)
+    pl.when(core != 0)(clear_all)
+
     group_row = lax.broadcasted_iota(jnp.int32, (group, wts.shape[3]), 0)
     turn_row = lax.broadcasted_iota(jnp.int32, (2 * width, width), 0)
     code_x = jnp.int32(coded([(SIDE - o[0]) % SIDE for o in ORDER]))

time: 40.3 us -> 40.8 us (1.012)
  Pallas kernels: 38.5 us -> 39 us
    pallas_call x1, Pallas kernels: 38.5 us -> 39 us  [on_device(): pl.pallas_call(kernel, out_shape=jax.ShapeDtypeStruct((tiles, rows, tile_...]
where the time goes in v6:
time: 40.8 us; the launch traced here: 40.6 us
  Pallas kernels  39 us (96%)
  local copies, waits for them, and re-layouts  0.88 us (2%)
  other arithmetic  0.72 us (2%)
    pallas_call x1, Pallas kernels, on_device(): pl.pallas_call(kernel, out_shape=jax.ShapeDtypeStruct((tiles, rows, tile_...  39 us
    unnamed x1, local copies, waits for them, and re-layouts  0.88 us

profile of v6, /device:TPU:0, one launch (start us, length us, event | category | flops | bytes accessed | tf_op | source)
XLA Modules:
  0.0 40.6 jit_solution(1577199101166667501)
XLA Ops:
  0.0 0.7 %pad_add_fusion.ints_in = s32[1,17,16]{2,1,0:T(8,128)S(1)} fusion(s32[1,1,16]{2,1,0:T(1,128)} %bitcast.5, s32[1,8,16]{2,1,0:T(8,128)} %bitcast.3, s32[1,8,16]{2,1,0:T(8,128)} %bitcast.4), kind=kLoop, calls=%fused_computation | loop fusion | flops 544 | bytes 2176 | tf_op jit(solution)/shard_map/concatenate | solution.py:405
  0.7 39.0 %shard_map.55 = f32[16,96,128]{2,1,0:T(8,128)S(1)} custom-call(s32[1,17,16]{2,1,0:T(8,128)S(1)} %pad_add_fusion.ints_in, f32[128,96,128]{2,1,0:T(8,128)} %fields_ref.1, bf16[1,16,8,384,128]{4,3,2,1,0:T(8,128)(2,1)} %weights_ref.1), custom_call_target="tpu_custom_call" | custom-call | flops 1208000000 | bytes 19700000 | tf_op jit(solution)/shard_map/pallas_call | solution.py:408
  39.7 0.9 %copy.7 = f32[16,96,128]{2,1,0:T(8,128)} copy(f32[16,96,128]{2,1,0:T(8,128)S(1)} %shard_map.55) | data formatting | bytes 1572864

commit v7 on v5

--- a/solution.py
+++ b/solution.py
@@ -128,15 +128,15 @@
 
     messages = []
 
-    def message(src, dst, peer):
-        i = len(messages)
-        messages.append(
-            pltpu.make_async_remote_copy(
-                src_ref=src, dst_ref=dst, send_sem=send_sem.at[i], recv_sem=recv_sem.at[i],
-                device_id=peer, device_id_type=MESH,
-            )
+    def message(src, dst, peer, i=None):
+        i = len(messages) if i is None else i
+        copy = pltpu.make_async_remote_copy(
+            src_ref=src, dst_ref=dst, send_sem=send_sem.at[i], recv_sem=recv_sem.at[i],
+            device_id=peer, device_id_type=MESH,
         )
-        return messages[i]
+        if i == len(messages):
+            messages.append(copy)
+        return copy
 
     halo = [
         message(fields_ref.at[bx - 1], cells.at[0], (up, blk)),
@@ -145,13 +145,17 @@
         message(col_send.at[1], col_recv.at[1], (face, left)),
     ]
     tables = [message(tab_send, tab_recv.at[i], near[name]) for i, name in enumerate(STEPS)]
-    raw, summed = {}, {}
+    raw, pieces, summed = {}, {}, {}
     for route, tree in enumerate(TREES):
         rs = pl.ds(route * height, height)
         for v in LEAVES[route]:
-            raw[route, v] = message(
-                part.at[ORDER.index(v), pl.ds(0, cap), rs], raw_in[route, v].at[pl.ds(0, cap)], near[tree[v]]
-            )
+            k = ORDER.index(v)
+            i = len(messages)
+            raw[route, v] = message(part.at[k, pl.ds(0, cap), rs], raw_in[route, v].at[pl.ds(0, cap)], near[tree[v]])
+            pieces[route, v] = [
+                message(part.at[k, pl.ds(c, 2), rs], raw_in[route, v].at[pl.ds(c, 2)], near[tree[v]], i)
+                for c in range(0, cap, 2)
+            ]
         for i, v in enumerate(INNER[route]):
             for h in range(PARTS):
                 some = pl.ds(h * share, share)
@@ -273,7 +277,8 @@
         part[0, c] = product.astype(part.dtype)
     for route in range(ROUTES):
         if ORDER[0] in LEAVES[route]:
-            raw[route, ORDER[0]].start()
+            for copy in pieces[route, ORDER[0]]:
+                copy.start()
 
     def read_tables():
         for copy in tables:
@@ -346,7 +351,7 @@
         for i, (o, sums_after) in enumerate(PLAN):
             if i == 0:
                 continue
-            ready = [raw[route, o] for route in range(ROUTES) if o in LEAVES[route]]
+            ready = [copy for route in range(ROUTES) if o in LEAVES[route] for copy in pieces[route, o]]
             if i == len(PLAN) - 1:
                 sums_after = ()
             if ready or sums_after or i == TABLES_AFTER:

time: 40.3 us -> 40.6 us (level)
  no operation moved by 1% of the time
where the time goes in v7:
time: 40.6 us; the launch traced here: 40.5 us
  Pallas kernels  38.9 us (96%)
  local copies, waits for them, and re-layouts  0.88 us (2%)
  other arithmetic  0.72 us (2%)
    pallas_call x1, Pallas kernels, on_device(): pl.pallas_call(kernel, out_shape=jax.ShapeDtypeStruct((tiles, rows, tile_...  38.9 us
    unnamed x1, local copies, waits for them, and re-layouts  0.88 us

profile of v7, /device:TPU:0, one launch (start us, length us, event | category | flops | bytes accessed | tf_op | source)
XLA Modules:
  0.0 40.5 jit_solution(16141202350867189894)
XLA Ops:
  0.0 0.7 %pad_add_fusion.ints_in = s32[1,17,16]{2,1,0:T(8,128)S(1)} fusion(s32[1,1,16]{2,1,0:T(1,128)} %bitcast.5, s32[1,8,16]{2,1,0:T(8,128)} %bitcast.3, s32[1,8,16]{2,1,0:T(8,128)} %bitcast.4), kind=kLoop, calls=%fused_computation | loop fusion | flops 544 | bytes 2176 | tf_op jit(solution)/shard_map/concatenate | solution.py:395
  0.7 38.9 %shard_map.55 = f32[16,96,128]{2,1,0:T(8,128)S(1)} custom-call(s32[1,17,16]{2,1,0:T(8,128)S(1)} %pad_add_fusion.ints_in, f32[128,96,128]{2,1,0:T(8,128)} %fields_ref.1, bf16[1,16,8,384,128]{4,3,2,1,0:T(8,128)(2,1)} %weights_ref.1), custom_call_target="tpu_custom_call" | custom-call | flops 1208000000 | bytes 19700000 | tf_op jit(solution)/shard_map/pallas_call | solution.py:398
  39.6 0.9 %copy.7 = f32[16,96,128]{2,1,0:T(8,128)} copy(f32[16,96,128]{2,1,0:T(8,128)S(1)} %shard_map.55) | data formatting | bytes 1572864

commit v8 on v5

--- a/solution.py
+++ b/solution.py
@@ -97,8 +97,10 @@
     blk = lax.axis_index("blk")
     px, py = blk // SIDE, lax.rem(blk, SIDE)
 
+    way = 1 - 2 * lax.rem(face, 2)
+
     def at(a, b):
-        return lax.rem(px + a, SIDE) * SIDE + lax.rem(py + b, SIDE)
+        return lax.rem(px + SIDE + way * a, SIDE) * SIDE + lax.rem(py + SIDE + way * b, SIDE)
 
     def writer(o):
         return at((SIDE - o[0]) % SIDE, (SIDE - o[1]) % SIDE)

time: 40.3 us -> 40.5 us (level)
  no operation moved by 1% of the time
where the time goes in v8:
time: 40.5 us; the launch traced here: 40.4 us
  Pallas kernels  38.8 us (96%)
  local copies, waits for them, and re-layouts  0.88 us (2%)
  other arithmetic  0.72 us (2%)
    pallas_call x1, Pallas kernels, on_device(): pl.pallas_call(kernel, out_shape=jax.ShapeDtypeStruct((tiles, rows, tile_...  38.8 us
    unnamed x1, local copies, waits for them, and re-layouts  0.88 us

profile of v8, /device:TPU:0, one launch (start us, length us, event | category | flops | bytes accessed | tf_op | source)
XLA Modules:
  0.0 40.4 jit_solution(2012911068719036251)
XLA Ops:
  0.0 0.7 %pad_add_fusion.ints_in = s32[1,17,16]{2,1,0:T(8,128)S(1)} fusion(s32[1,1,16]{2,1,0:T(1,128)} %bitcast.5, s32[1,8,16]{2,1,0:T(8,128)} %bitcast.3, s32[1,8,16]{2,1,0:T(8,128)} %bitcast.4), kind=kLoop, calls=%fused_computation | loop fusion | flops 544 | bytes 2176 | tf_op jit(solution)/shard_map/concatenate | solution.py:392
  0.7 38.8 %shard_map.55 = f32[16,96,128]{2,1,0:T(8,128)S(1)} custom-call(s32[1,17,16]{2,1,0:T(8,128)S(1)} %pad_add_fusion.ints_in, f32[128,96,128]{2,1,0:T(8,128)} %fields_ref.1, bf16[1,16,8,384,128]{4,3,2,1,0:T(8,128)(2,1)} %weights_ref.1), custom_call_target="tpu_custom_call" | custom-call | flops 1208000000 | bytes 19700000 | tf_op jit(solution)/shard_map/pallas_call | solution.py:395
  39.5 0.9 %copy.7 = f32[16,96,128]{2,1,0:T(8,128)} copy(f32[16,96,128]{2,1,0:T(8,128)S(1)} %shard_map.55) | data formatting | bytes 1572864
